TPU v7x, 256 devices: a whole 4x4x8 slice. The times are simulated.
256 devices in a mesh: seq: 32 (over z, y), head: 8 (over x, core).
Axes of the slice: x: 4, y: 4, z: 8, core: 2. Of those that a mesh axis runs over, the one named last changes fastest.
Arguments:
- queries: bfloat16 [16384, 8192], P('seq', 'head'), may hold values from -6 to 6
- keys: bfloat16 [16384, 8192], P('seq', 'head'), may hold values from -6 to 6
- values: bfloat16 [16384, 8192], P('seq', 'head'), may hold values from -10 to 10
- norm_gain: float32 [8192], P('head'), may hold values from 0.1 to 1.9
- out_grad: bfloat16 [16384, 8192], P('seq', 'head'), may hold values from -6 to 6
Outputs:
- normed: bfloat16 [16384, 8192], P('seq', 'head')
- query_grad: bfloat16 [16384, 8192], P('seq', 'head')
- key_grad: bfloat16 [16384, 8192], P('seq', 'head')
- value_grad: bfloat16 [16384, 8192], P('seq', 'head')
All inputs are finite; a program needn't handle non-finite values.
Results may differ from a plain program's by a relative error of at most 0.0058.
Values sent between devices are 32-bit elements; how exact they have to be, the bound alone decides.
A program may use at most 128 MiB of HBM per device.

v0:
```python
import jax
import jax.numpy as jnp
from jax import lax
from jax.sharding import PartitionSpec as P

HD = 128
BLK = 512


def entering(array, axis, combine, identity, reverse):
    count, mine = (lax.axis_size(axis), lax.axis_index(axis))
    everything = lax.all_gather(array, axis)
    start = jnp.broadcast_to(jnp.asarray(identity, array.dtype), array.shape)

    def hop(k, before):
        at = count - 1 - k if reverse else k
        reached = at > mine if reverse else at < mine
        new = combine(before, everything[at])
        return jnp.where(reached, new, before)

    return lax.fori_loop(0, count, hop, start)


def add_states(first, second):
    return first + second


def earlier_states(total):
    return entering(total, "seq", add_states, jnp.zeros_like(total), False)


def later_states(total):
    return entering(total, "seq", add_states, jnp.zeros_like(total), True)


def local(queries, keys, values, norm_gain, out_grad):
    tok_rows, width = queries.shape
    count = tok_rows // BLK
    scale = HD ** (-0.5)
    full_width = width * lax.axis_size("head")
    lower = jnp.tril(jnp.ones((BLK, BLK), dtype=bool))
    heads_here = width // HD
    shape4 = (count, BLK, heads_here, HD)
    query_b = queries.reshape(shape4)
    key_b = keys.reshape(shape4)
    value_b = values.reshape(shape4)
    block_kv = jnp.einsum("nshd,nshe->nhde", key_b, value_b, preferred_element_type=jnp.float32)
    inside = jnp.cumsum(block_kv, axis=0) - block_kv
    before = earlier_states(jnp.sum(block_kv, axis=0))
    state_bf = (before[None] + inside).astype(jnp.bfloat16)
    raw = jnp.einsum("nthd,nshd->nhts", query_b, key_b, preferred_element_type=jnp.float32) * scale
    scores = jnp.where(lower[None, None], raw, 0.0).astype(jnp.bfloat16)
    attended = jnp.einsum("nhts,nshe->nthe", scores, value_b, preferred_element_type=jnp.float32)
    attended = attended + scale * jnp.einsum(
        "nthd,nhde->nthe", query_b, state_bf, preferred_element_type=jnp.float32
    )
    flat = attended.reshape(tok_rows, width)
    grad_norm = out_grad.astype(jnp.float32) * norm_gain[None, :]
    squares = lax.psum(jnp.sum(flat * flat, axis=1), "head")
    rms = jnp.sqrt(squares / full_width + 1e-06)[:, None]
    unit = flat / rms
    products = lax.psum(jnp.sum(grad_norm * unit, axis=1), "head")
    proj = (products / full_width)[:, None]
    normed = (unit * norm_gain[None, :]).astype(jnp.bfloat16)
    att_grad = ((grad_norm - unit * proj) / rms).astype(jnp.bfloat16)
    grad_b = att_grad.reshape(shape4)
    block_qg = jnp.einsum("nthd,nthe->nhde", query_b, grad_b, preferred_element_type=jnp.float32)
    total_qg = jnp.sum(block_qg, axis=0)
    behind = total_qg[None] - jnp.cumsum(block_qg, axis=0)
    after = later_states(total_qg)
    later_bf = (after[None] + behind).astype(jnp.bfloat16)
    graw = jnp.einsum("nthe,nshe->nhts", grad_b, value_b, preferred_element_type=jnp.float32)
    gscores = jnp.where(lower[None, None], graw, 0.0).astype(jnp.bfloat16)
    qgrad = jnp.einsum("nhts,nshd->nthd", gscores, key_b, preferred_element_type=jnp.float32)
    qgrad = scale * (
        qgrad + jnp.einsum("nthe,nhde->nthd", grad_b, state_bf, preferred_element_type=jnp.float32)
    )
    kgrad = jnp.einsum("nhts,nthd->nshd", gscores, query_b, preferred_element_type=jnp.float32)
    kgrad = scale * (
        kgrad + jnp.einsum("nshe,nhde->nshd", value_b, later_bf, preferred_element_type=jnp.float32)
    )
    vgrad = jnp.einsum("nhts,nthe->nshe", scores, grad_b, preferred_element_type=jnp.float32)
    vgrad = vgrad + scale * jnp.einsum(
        "nshd,nhde->nshe", key_b, later_bf, preferred_element_type=jnp.float32
    )
    return (
        normed,
        qgrad.reshape(tok_rows, width).astype(jnp.bfloat16),
        kgrad.reshape(tok_rows, width).astype(jnp.bfloat16),
        vgrad.reshape(tok_rows, width).astype(jnp.bfloat16),
    )


def solution(mesh):
    placed = (P("seq", "head"), P("seq", "head"), P("seq", "head"), P("head"), P("seq", "head"))
    return jax.shard_map(
        local,
        mesh=mesh,
        in_specs=placed,
        out_specs=(P("seq", "head"), P("seq", "head"), P("seq", "head"), P("seq", "head")),
        check_vma=False,
    )
```

profile of v0, /device:TPU:8, one launch (start us, length us, event | category | flops | bytes accessed | tf_op | source)
XLA Modules:
  0.0 428.4 jit_solution(13384025313433181688)
XLA Ops:
  7.2 1.6 copy.63
  9.5 1.3 fusion.9
  11.7 4.6 %select_convert_fusion.1 = bf16[8,512,512]{2,1,0:T(8,128)(2,1)} fusion(pred[512,512]{1,0:T(8,128)(4,1)S(1)} %iota_compare_fusion, bf16[512,1024]{1,0:T(8,128)(2,1)} %param.10, bf16[512,1024]{1,0:T(8,128)(2,1)S(1)} %copy-done.3), kind=kOutput, calls=%fused_computation.3 | convolution fusion | flops 543162368 | bytes 6553600 | tf_op jit(solution)/shard_map/nthd,nshd->nhts/dot_general | solution.py:51
  16.2 137.2 %all-gather.5.cloned.1.call-done = f32[256,128,128]{2,1,0:T(8,128)} async-done(((f32[8,128,128]{2,1,0:T(8,128)}), f32[256,128,128]{2,1,0:T(8,128)}) %all-gather.5.cloned.1.call-update) | async-done | bytes 16777232 | tf_op jit(solution)/shard_map/all_gather | solution.py:12
  153.4 40.1 %while.30 = (s32[]{:T(128)}, f32[8,128,128]{2,1,0:T(8,128)S(1)}, s32[]{:T(128)}, f32[32,8,128,128]{3,2,1,0:T(8,128)}, s32[]{:T(128)}, /*index=5*/s32[]{:T(128)}) while((s32[]{:T(128)}, f32[8,128,128]{2,1,0:T(8,128)S(1)}, s32[]{:T(128)}, f32[32,8,128,128]{3,2,1,0:T(8,128)}, s32[]{:T(128)}, /*index=5*/s32[]{:T(128)}) %tuple.87), condition=%wide.region_1.2_spmd.clone, body=%wide.region_0.1_spmd.clone.sunk | while | flops 393220 | bytes 1572965 | solution.py:21
  153.4 1.3 add_select_fusion.4
  154.7 1.2 add_select_fusion.4
  156.0 1.2 add_select_fusion.4
  157.2 1.2 add_select_fusion.4
  158.5 1.2 add_select_fusion.4
  159.7 1.2 add_select_fusion.4
  161.0 1.2 add_select_fusion.4
  162.2 1.2 add_select_fusion.4
  163.5 1.2 add_select_fusion.4
  164.7 1.2 add_select_fusion.4
  166.0 1.2 add_select_fusion.4
  167.2 1.2 add_select_fusion.4
  168.5 1.2 add_select_fusion.4
  169.7 1.2 add_select_fusion.4
  171.0 1.2 add_select_fusion.4
  172.2 1.2 add_select_fusion.4
  173.5 1.2 add_select_fusion.4
  174.8 1.2 add_select_fusion.4
  176.0 1.2 add_select_fusion.4
  177.3 1.2 add_select_fusion.4
  178.5 1.2 add_select_fusion.4
  179.8 1.2 add_select_fusion.4
  181.0 1.2 add_select_fusion.4
  182.3 1.2 add_select_fusion.4
  183.5 1.2 add_select_fusion.4
  184.8 1.2 add_select_fusion.4
  186.0 1.2 add_select_fusion.4
  187.3 1.2 add_select_fusion.4
  188.5 1.2 add_select_fusion.4
  189.8 1.2 add_select_fusion.4
  191.0 1.2 add_select_fusion.4
  192.3 1.2 add_select_fusion.4
  194.1 1.6 copy-done.1
  195.7 2.9 fusion.4
  198.6 14.1 %psum.14 = f32[512]{0:T(512)S(1)} all-reduce(f32[512]{0:T(512)S(1)} %get-tuple-element.255), channel_id=1, replica_groups=mesh['seq'=32,'head'=8] {'head'}, use_global_device_ids=true, to_apply=%region_3.4 | all-reduce | flops 512 | bytes 4096 | tf_op jit(solution)/shard_map/psum | solution.py:59
  212.7 1.9 copy.40
  214.7 1.7 multiply_reduce_fusion
  216.3 12.6 %psum.15 = f32[512]{0:T(512)S(1)} all-reduce(f32[512]{0:T(512)S(1)} %multiply_reduce_fusion), channel_id=1, replica_groups=mesh['seq'=32,'head'=8] {'head'}, use_global_device_ids=true, to_apply=%region_5.6 | all-reduce | flops 512 | bytes 4096 | tf_op jit(solution)/shard_map/psum | solution.py:62
  228.9 3.1 divide_convert_fusion
  232.1 1.5 copy.59
  233.6 1.7 convolution_bitcast_fusion
  237.3 1.4 select_convert_fusion
  238.7 2.5 fusion.3
  241.2 2.3 copy.54
  243.4 4.6 %fusion.29 = f32[8,128,512]{2,1,0:T(8,128)} fusion(bf16[512,8,128]{0,2,1:T(8,128)(2,1)S(1)} %bitcast.127, bf16[8,512,512]{2,1,0:T(8,128)(2,1)} %select_convert_fusion.1), kind=kOutput, calls=%fused_computation.49 | convolution fusion | flops 536870912 | bytes 7340032 | tf_op jit(solution)/shard_map/nhts,nthe->nshe/dot_general | solution.py:82
  248.0 123.7 %all-gather.7.cloned.1.call-done = f32[256,128,128]{2,1,0:T(8,128)} async-done(((f32[8,128,128]{2,1,0:T(8,128)}), f32[256,128,128]{2,1,0:T(8,128)}) %all-gather.7.cloned.1.call-update) | async-done | bytes 16777232 | tf_op jit(solution)/shard_map/all_gather | solution.py:12
  371.7 40.2 %while.31 = (s32[]{:T(128)}, f32[8,128,128]{2,1,0:T(8,128)S(1)}, s32[]{:T(128)}, f32[32,8,128,128]{3,2,1,0:T(8,128)}, s32[]{:T(128)}, /*index=5*/s32[]{:T(128)}, s32[]{:T(128)}, s32[]{:T(128)}) while((s32[]{:T(128)}, f32[8,128,128]{2,1,0:T(8,128)S(1)}, s32[]{:T(128)}, f32[32,8,128,128]{3,2,1,0:T(8,128)}, s32[]{:T(128)}, ...), condition=%wide.region_7.8_spmd.clone, body=%wide.region_6.7_spmd.clone.sunk | while | flops 393224 | bytes 1573027 | solution.py:21
  373.0 1.2 add_select_fusion.5
  374.2 1.2 add_select_fusion.5
  375.5 1.2 add_select_fusion.5
  376.7 1.2 add_select_fusion.5
  378.0 1.2 add_select_fusion.5
  379.3 1.2 add_select_fusion.5
  399.4 1.2 add_select_fusion.5
  401.9 1.2 add_select_fusion.5
  412.2 1.8 fusion.6
  415.2 1.3 copy.56
  416.5 3.7 fusion.1
  420.2 1.3 copy.55
  (66 shorter events, 35.0 us)
Async XLA Ops:
  7.2 2.3 copy-start
  7.2 146.2 %all-gather.5.cloned.1.call-start = ((), (), s32[]{:S(2)}) async-start(), calls=%async_computation | async-start | bytes 17301504 | tf_op jit(solution)/shard_map/all_gather | solution.py:12
  9.5 1.4 copy-start.5
  9.5 2.2 copy-start.3
  10.8 360.9 %all-gather.7.cloned.1.call-start = ((), (), s32[]{:S(2)}) async-start(), calls=%async_computation.1 | async-start | bytes 17301504 | tf_op jit(solution)/shard_map/all_gather | solution.py:12
  11.0 0.7 copy-start.10
  153.4 40.1 %copy-start.8 = (f32[8,128,128]{2,1,0:T(8,128)S(1)}, f32[8,128,128]{2,1,0:T(8,128)}, u32[]{:S(2)}) copy-start(f32[8,128,128]{2,1,0:T(8,128)} %fusion.9) | copy-start | bytes 1572868
  193.5 2.2 copy-start.1
  212.7 1.9 copy-start.12
  236.3 1.0 copy-start.11
  237.3 1.4 copy-start.6
  238.7 2.5 copy-start.2
  412.1 1.9 copy-start.7
  412.1 2.6 copy-start.9
  415.2 1.3 copy-start.4
Sparse Core Ops, SparseCore 0:
  11.2 142.2 all-gather.4
  236.4 135.2 all-gather.6
where the time goes:
time: 434 us; the launch traced here: 428 us
  waiting for transfers between devices  261 us (60%)
  other arithmetic  83.6 us (19%)
  blocking collectives  26.7 us (6%)
  matrix products  25.7 us (6%)
  local copies, waits for them, and re-layouts  15.4 us (4%)
  between operations  14.3 us (3%)
    all_gather x2, waiting for transfers between devices, entering(): everything = lax.all_gather(array, axis)  261 us
    select_n x64, other arithmetic, hop(): return jnp.where(reached, new, before)  78.6 us
    psum x1, blocking collectives, local(): squares = lax.psum(jnp.sum(flat * flat, axis=1), 'head')  14.1 us
    psum x1, blocking collectives, local(): products = lax.psum(jnp.sum(grad_norm * unit, axis=1), 'head')  12.6 us
    unnamed x30, local copies, waits for them, and re-layouts  10.1 us
  transfers between devices with their start and end apart: 2, of which 2 were waited for; matrix products, arithmetic and copies ran while one was open for 4% of the time, Pallas kernels for 0%

commit v1 on v0

v1 whole, which is shorter than its diff:
```python
import functools

import jax
import jax.numpy as jnp
from jax import lax
from jax.experimental import pallas as pl
from jax.experimental.pallas import tpu as pltpu
from jax.sharding import PartitionSpec as P

HD = 128
BLK = 512
NY = 4
CHUNKS = 2
HALF = BLK // 2
F32 = jnp.float32
BF16 = jnp.bfloat16
MESH = pl.DeviceIdType.MESH
EXACT = lax.Precision.HIGHEST


def dot_nn(a, b):
    return lax.dot_general(a, b, (((1,), (0,)), ((), ())), preferred_element_type=F32)


def dot_nt(a, b):
    return lax.dot_general(a, b, (((1,), (1,)), ((), ())), preferred_element_type=F32)


def dot_tn(a, b):
    return lax.dot_general(a, b, (((0,), (0,)), ((), ())), preferred_element_type=F32)


def exact_nt(a, b):
    return lax.dot_general(a, b, (((1,), (1,)), ((), ())), precision=EXACT, preferred_element_type=F32)


def exact_tn(a, b):
    return lax.dot_general(a, b, (((0,), (0,)), ((), ())), precision=EXACT, preferred_element_type=F32)


class Scan:
    def __init__(self, nz, rows, reverse, refs, sems):
        self.nz, self.rows, self.reverse = nz, rows, reverse
        self.block, self.b1, self.tot, self.b2, self.pre, self.b3, self.ret, self.b4 = refs
        self.ysend, self.yrecv, self.zsend, self.zrecv = sems
        seq = lax.axis_index("seq")
        self.head = lax.axis_index("head")
        self.z, self.y = lax.div(seq, NY), lax.rem(seq, NY)
        self.quarter = rows // NY
        self.piece = self.quarter // nz
        self.sends = []

    def y_copy(self, phase, c, d, src, dst):
        k = (phase * CHUNKS + c) * (NY - 1) + d - 1
        to = self.z * NY + lax.rem(self.y + d, NY)
        return pltpu.make_async_remote_copy(
            src_ref=src, dst_ref=dst, send_sem=self.ysend.at[k], recv_sem=self.yrecv.at[k],
            device_id=(to, self.head), device_id_type=MESH,
        )

    def z_copy(self, phase, c, d, src, dst):
        k = (phase * CHUNKS + c) * (self.nz - 1) + d - 1
        to = lax.rem(self.z + d, self.nz) * NY + self.y
        return pltpu.make_async_remote_copy(
            src_ref=src, dst_ref=dst, send_sem=self.zsend.at[k], recv_sem=self.zrecv.at[k],
            device_id=(to, self.head), device_id_type=MESH,
        )

    def begin(self, copies):
        for copy in copies:
            copy.start()
        self.sends += copies
        return copies

    def y_out(self, c):
        base = c * self.rows

        def part(q):
            return self.block.at[pl.ds(pl.multiple_of(base + q * self.quarter, 8), self.quarter)]

        copies = self.begin([
            self.y_copy(0, c, d, part(lax.rem(self.y + d, NY)), self.b1.at[c, self.y]) for d in (2, 1, 3)
        ])
        self.b1[c, self.y] = part(self.y)[...]
        return copies

    def z_out(self, c, arriving):
        for copy in arriving:
            copy.wait_recv()
        self.tot[c] = (self.b1[c, 0] + self.b1[c, 1]) + (self.b1[c, 2] + self.b1[c, 3])

        def part(j):
            return self.tot.at[c, pl.ds(pl.multiple_of(j * self.piece, 8), self.piece)]

        far = sorted(range(1, self.nz), key=lambda d: -min(d, self.nz - d))
        copies = self.begin([
            self.z_copy(0, c, d, part(lax.rem(self.z + d, self.nz)), self.b2.at[c, self.z]) for d in far
        ])
        self.b2[c, self.z] = part(self.z)[...]
        return copies

    def z_back(self, c, arriving):
        for copy in arriving:
            copy.wait_recv()
        order = range(self.nz)
        total = jnp.zeros((self.piece, HD), F32)
        for j in reversed(order) if self.reverse else order:
            self.pre[c, j] = total
            total = total + self.b2[c, j]
        far = sorted(range(1, self.nz), key=lambda d: -min(d, self.nz - d))
        copies = self.begin([
            self.z_copy(1, c, d, self.pre.at[c, lax.rem(self.z + d, self.nz)], self.b3.at[c, self.z]) for d in far
        ])
        self.b3[c, self.z] = self.pre[c, self.z]
        return copies

    def y_back(self, c, arriving):
        for copy in arriving:
            copy.wait_recv()
        total = self.b3[c].reshape(self.quarter, HD)
        order = range(NY)
        for j in reversed(order) if self.reverse else order:
            self.ret[c, j] = total
            total = total + self.b1[c, j]
        copies = self.begin([
            self.y_copy(1, c, d, self.ret.at[c, lax.rem(self.y + d, NY)], self.b4.at[c, self.y]) for d in (2, 1, 3)
        ])
        self.b4[c, self.y] = self.ret[c, self.y]
        return copies

    def finish(self):
        for copy in self.sends:
            copy.wait_send()


def kernel(nz, nh, heads, q_hbm, k_hbm, v_hbm, gain_hbm, g_hbm, normed_hbm, qgrad_hbm, kgrad_hbm, vgrad_hbm,
           q, k, v, gain, g, scores, att, dout, kpart, vpart, normed, qgrad, kgrad, vgrad, state_bf, squares,
           products, inv_b, coef_b, head_src, head_dst, *rest):
    fwd_refs, bwd_refs = rest[0:8], rest[8:16]
    fwd_sems, bwd_sems = rest[16:20], rest[20:24]
    in_sem, out_sem, head_send, head_recv = rest[24:28]
    later_bf = rest[28]
    scale = HD ** (-0.5)
    per = heads // CHUNKS
    rows = per * HD
    width = heads * HD
    seq, head = lax.axis_index("seq"), lax.axis_index("head")
    z, y = lax.div(seq, NY), lax.rem(seq, NY)

    barrier = pltpu.get_barrier_semaphore()
    for d in range(1, NY):
        to = z * NY + lax.rem(y + d, NY)
        pl.semaphore_signal(barrier, inc=1, device_id=(to, head), device_id_type=MESH)
    for d in range(1, nz):
        to = lax.rem(z + d, nz) * NY + y
        pl.semaphore_signal(barrier, inc=1, device_id=(to, head), device_id_type=MESH)
    for d in range(1, nh):
        pl.semaphore_signal(barrier, inc=1, device_id=(seq, lax.rem(head + d, nh)), device_id_type=MESH)

    loads = []
    for c in range(CHUNKS):
        cols = pl.ds(c * rows, rows)
        pair = []
        for i, (src, dst) in enumerate(((k_hbm, k), (v_hbm, v))):
            copy = pltpu.make_async_copy(src.at[:, cols], dst.at[:, cols], in_sem.at[2 * c + i])
            copy.start()
            pair.append(copy)
        loads.append(pair)
    late = []
    for i, (src, dst) in enumerate(((q_hbm, q), (g_hbm, g), (gain_hbm, gain))):
        copy = pltpu.make_async_copy(src, dst, in_sem.at[2 * CHUNKS + i])
        copy.start()
        late.append(copy)

    fwd = Scan(nz, rows, False, fwd_refs, fwd_sems)
    bwd = Scan(nz, rows, True, bwd_refs, bwd_sems)

    def lanes(h):
        return pl.ds(pl.multiple_of(h * HD, HD), HD)

    def sub(h):
        return pl.ds(pl.multiple_of(h * HD, HD), HD)

    def each(first, count, body):
        def step(h, _):
            body(h)
            return 0

        lax.fori_loop(first, first + count, step, 0)

    def kv(h):
        fwd.block[sub(h), :] = dot_tn(k[:, lanes(h)], v[:, lanes(h)])

    moving = []
    for c in range(CHUNKS):
        for copy in loads[c]:
            copy.wait()
        each(c * per, per, kv)
        if c == 0:
            pl.semaphore_wait(barrier, (NY - 1) + (nz - 1) + (nh - 1))
        moving.append(fwd.y_out(c))
    for copy in late:
        copy.wait()

    causal = lax.broadcasted_iota(jnp.int32, (HALF, HALF), 0) >= lax.broadcasted_iota(jnp.int32, (HALF, HALF), 1)

    def tiles(a, b, factor):
        top = jnp.where(causal, dot_nt(a[:HALF], b[:HALF]) * factor, 0.0).astype(BF16)
        low = (dot_nt(a[HALF:], b[:HALF]) * factor).astype(BF16)
        end = jnp.where(causal, dot_nt(a[HALF:], b[HALF:]) * factor, 0.0).astype(BF16)
        return top, low, end

    def intra(h):
        vh = v[:, lanes(h)]
        top, low, end = tiles(q[:, lanes(h)], k[:, lanes(h)], scale)
        scores[h, 0], scores[h, 1], scores[h, 2] = top, low, end
        att[:HALF, lanes(h)] = dot_nn(top, vh[:HALF])
        att[HALF:, lanes(h)] = dot_nn(low, vh[:HALF]) + dot_nn(end, vh[HALF:])

    each(0, heads // 2, intra)
    for c in range(CHUNKS):
        moving[c] = fwd.z_out(c, moving[c])
    each(heads // 2, heads - heads // 2, intra)
    for c in range(CHUNKS):
        moving[c] = fwd.z_back(c, moving[c])
    squares[...] = jnp.zeros_like(squares)
    products[...] = jnp.zeros_like(products)
    for c in range(CHUNKS):
        moving[c] = fwd.y_back(c, moving[c])

    for c in range(CHUNKS):
        for copy in moving[c]:
            copy.wait_recv()
        state_bf[pl.ds(c * rows, rows), :] = fwd.b4[c].reshape(rows, HD).astype(BF16)

        def attend(h):
            a = att[:, lanes(h)] + scale * dot_nn(q[:, lanes(h)], state_bf[sub(h), :])
            att[:, lanes(h)] = a
            squares[...] += a * a
            products[...] += a * (g[:, lanes(h)].astype(F32) * gain[:, lanes(h)])

        each(c * per, per, attend)

    row = lax.broadcasted_iota(jnp.int32, (8, HD), 0)
    groups = BLK // HD
    packed = jnp.zeros((8, HD), F32)
    for t in range(groups):
        part = pl.ds(t * HD, HD)
        packed = packed + exact_nt((row == t).astype(F32), squares[part, :])
        packed = packed + exact_nt((row == groups + t).astype(F32), products[part, :])
    head_src[...] = packed
    head_copies = []
    for d in range(1, nh):
        copy = pltpu.make_async_remote_copy(
            src_ref=head_src, dst_ref=head_dst.at[head], send_sem=head_send.at[d - 1], recv_sem=head_recv.at[d - 1],
            device_id=(seq, lax.rem(head + d, nh)), device_id_type=MESH,
        )
        copy.start()
        head_copies.append(copy)
    head_dst[head] = packed
    for copy in head_copies:
        copy.wait_recv()
    sums = head_dst[0]
    for j in range(1, nh):
        sums = sums + head_dst[j]
    full = nh * width
    inv = 1.0 / jnp.sqrt(sums[:groups] / full + 1e-06)
    proj = (sums[groups:] * inv) / full
    both = jnp.concatenate([inv, (inv * proj) * inv], axis=0)
    for t in range(groups):
        part = pl.ds(t * HD, HD)
        inv_b[part, :] = exact_tn(both, (row == t).astype(F32))
        coef_b[part, :] = exact_tn(both, (row == groups + t).astype(F32))

    def grad(h):
        gn = g[:, lanes(h)].astype(F32) * gain[:, lanes(h)]
        d = (gn * inv_b[...] - att[:, lanes(h)] * coef_b[...]).astype(BF16)
        dout[:, lanes(h)] = d
        bwd.block[sub(h), :] = dot_tn(q[:, lanes(h)], d)

    for c in range(CHUNKS):
        each(c * per, per, grad)
        moving[c] = bwd.y_out(c)

    def back(h):
        qh, kh, vh, d = q[:, lanes(h)], k[:, lanes(h)], v[:, lanes(h)], dout[:, lanes(h)]
        normed[:, lanes(h)] = (att[:, lanes(h)] * inv_b[...] * gain[:, lanes(h)]).astype(BF16)
        top, low, end = tiles(d, vh, 1.0)
        carried = dot_nt(d, state_bf[sub(h), :])
        qgrad[:HALF, lanes(h)] = (scale * (dot_nn(top, kh[:HALF]) + carried[:HALF])).astype(BF16)
        qgrad[HALF:, lanes(h)] = (
            scale * (dot_nn(low, kh[:HALF]) + dot_nn(end, kh[HALF:]) + carried[HALF:])
        ).astype(BF16)
        kpart[:HALF, lanes(h)] = dot_tn(top, qh[:HALF]) + dot_tn(low, qh[HALF:])
        kpart[HALF:, lanes(h)] = dot_tn(end, qh[HALF:])
        vpart[:HALF, lanes(h)] = dot_tn(scores[h, 0], d[:HALF]) + dot_tn(scores[h, 1], d[HALF:])
        vpart[HALF:, lanes(h)] = dot_tn(scores[h, 2], d[HALF:])

    outs = []

    def put(src, dst):
        copy = pltpu.make_async_copy(src, dst, out_sem.at[len(outs)])
        copy.start()
        outs.append(copy)

    each(0, heads // 2, back)
    for c in range(CHUNKS):
        moving[c] = bwd.z_out(c, moving[c])
    each(heads // 2, heads - heads // 2, back)
    for c in range(CHUNKS):
        moving[c] = bwd.z_back(c, moving[c])
    put(normed, normed_hbm)
    put(qgrad, qgrad_hbm)
    for c in range(CHUNKS):
        moving[c] = bwd.y_back(c, moving[c])
    for c in range(CHUNKS):
        for copy in moving[c]:
            copy.wait_recv()

        def last(h):
            here = later_bf[sub(h), :]
            kgrad[:, lanes(h)] = (scale * (kpart[:, lanes(h)] + dot_nt(v[:, lanes(h)], here))).astype(BF16)
            vgrad[:, lanes(h)] = (vpart[:, lanes(h)] + scale * dot_nn(k[:, lanes(h)], here)).astype(BF16)

        later_bf[pl.ds(c * rows, rows), :] = bwd.b4[c].reshape(rows, HD).astype(BF16)
        each(c * per, per, last)
        cols = pl.ds(c * rows, rows)
        put(kgrad.at[:, cols], kgrad_hbm.at[:, cols])
        put(vgrad.at[:, cols], vgrad_hbm.at[:, cols])

    fwd.finish()
    for copy in head_copies:
        copy.wait_send()
    bwd.finish()
    for copy in outs:
        copy.wait()


def local(queries, keys, values, norm_gain, out_grad):
    blk, width = queries.shape
    heads = width // HD
    nz = lax.axis_size("seq") // NY
    nh = lax.axis_size("head")
    rows = heads // CHUNKS * HD
    quarter = rows // NY
    piece = quarter // nz
    vmem = pltpu.VMEM

    def scan_refs():
        return [
            vmem((heads * HD, HD), F32),
            vmem((CHUNKS, NY, quarter, HD), F32),
            vmem((CHUNKS, quarter, HD), F32),
            vmem((CHUNKS, nz, piece, HD), F32),
            vmem((CHUNKS, nz, piece, HD), F32),
            vmem((CHUNKS, nz, piece, HD), F32),
            vmem((CHUNKS, NY, quarter, HD), F32),
            vmem((CHUNKS, NY, quarter, HD), F32),
        ]

    def scan_sems():
        y, zz = 2 * CHUNKS * (NY - 1), 2 * CHUNKS * (nz - 1)
        dma = pltpu.SemaphoreType.DMA
        return [dma((y,)), dma((y,)), dma((zz,)), dma((zz,))]

    big_f32, big_bf16 = vmem((blk, width), F32), vmem((blk, width), BF16)
    scratch = [
        big_bf16, big_bf16, big_bf16, vmem((1, width), F32), big_bf16,
        vmem((heads, 3, HALF, HALF), BF16),
        big_f32, big_bf16, big_f32, big_f32,
        big_bf16, big_bf16, big_bf16, big_bf16,
        vmem((heads * HD, HD), BF16),
        vmem((blk, HD), F32), vmem((blk, HD), F32), vmem((blk, HD), F32), vmem((blk, HD), F32),
        vmem((8, HD), F32), vmem((nh, 8, HD), F32),
        *scan_refs(), *scan_refs(), *scan_sems(), *scan_sems(),
        pltpu.SemaphoreType.DMA((2 * CHUNKS + 3,)),
        pltpu.SemaphoreType.DMA((2 + 2 * CHUNKS,)),
        pltpu.SemaphoreType.DMA((nh - 1,)),
        pltpu.SemaphoreType.DMA((nh - 1,)),
        vmem((heads * HD, HD), BF16),
    ]
    out = jax.ShapeDtypeStruct((blk, width), BF16)
    return pl.pallas_call(
        functools.partial(kernel, nz, nh, heads),
        out_shape=(out, out, out, out),
        in_specs=[pl.BlockSpec(memory_space=pl.ANY)] * 5,
        out_specs=(pl.BlockSpec(memory_space=pl.ANY),) * 4,
        scratch_shapes=scratch,
        compiler_params=pltpu.CompilerParams(
            collective_id=0, has_side_effects=True, vmem_limit_bytes=56 * 1024 * 1024
        ),
        name="linear_attention",
    )(queries, keys, values, norm_gain.reshape(1, width), out_grad)


def solution(mesh):
    placed = (P("seq", "head"), P("seq", "head"), P("seq", "head"), P("head"), P("seq", "head"))
    return jax.shard_map(
        local,
        mesh=mesh,
        in_specs=placed,
        out_specs=(P("seq", "head"), P("seq", "head"), P("seq", "head"), P("seq", "head")),
        check_vma=False,
    )
```

time: 434 us -> 72 us (0.17); the launches traced: 428 us -> 71.8 us
  waiting for transfers between devices: 261 us -> 0 us
  other arithmetic: 83.6 us -> 0 us
  Pallas kernels: 0 us -> 64.6 us
  blocking collectives: 26.7 us -> 0 us
  matrix products: 25.7 us -> 0 us
  between operations: 14.3 us -> 0.65 us
  local copies, waits for them, and re-layouts: 15.4 us -> 6.53 us
    all_gather x2 -> x0, waiting for transfers between devices: 261 us -> none  [entering(): everything = lax.all_gather(array, axis)]
    select_n x64 -> x0, other arithmetic: 78.6 us -> none  [hop(): return jnp.where(reached, new, before)]
    pallas_call x0 -> x1, Pallas kernels: none -> 64.6 us  [local(): pl.pallas_call(functools.partial(kernel, nz, nh, heads), out_shape=(out,...]
    psum x2 -> x0, blocking collectives: 26.7 us -> none  [the longest x1 14.1 us: local(): squares = lax.psum(jnp.sum(flat * flat, axis=1), 'head')]
    dot_general x12 -> x0, matrix products: 25.7 us -> none  [the longest x1 4.57 us: local(): jnp.einsum('nhts,nthe->nshe', scores, grad_b, preferred_element_type=jnp....]
    unnamed x30 -> x10, local copies, waits for them, and re-layouts: 10.1 us -> 6.53 us
  transfers between devices with their start and end apart: 2 -> 0, of which waited for: 2 -> 0; matrix products, arithmetic and copies ran while one was open for 4% -> 0% of each run, Pallas kernels for 0% -> 0%
where the time goes in v1:
time: 72 us; the launch traced here: 71.8 us
  Pallas kernels  64.6 us (90%)
  local copies, waits for them, and re-layouts  6.53 us (9%)
    pallas_call x1, Pallas kernels, local(): pl.pallas_call(functools.partial(kernel, nz, nh, heads), out_shape=(out,...  64.6 us
    unnamed x10, local copies, waits for them, and re-layouts  6.53 us

profile of v1, /device:TPU:8, one launch (start us, length us, event | category | flops | bytes accessed | tf_op | source)
XLA Modules:
  0.0 71.8 jit_solution(7302583736452559356)
XLA Ops:
  0.6 64.6 %linear_attention.1 = (bf16[512,1024]{1,0:T(8,128)(2,1)}, bf16[512,1024]{1,0:T(8,128)(2,1)}, bf16[512,1024]{1,0:T(8,128)(2,1)}, bf16[512,1024]{1,0:T(8,128)(2,1)}) custom-call(bf16[512,1024]{1,0:T(8,128)(2,1)} %q_hbm.1, bf16[512,1024]{1,0:T(8,128)(2,1)} %k_hbm.1, bf16[512,1024]{1,0:T(8,128)(2,1)} %v_hbm.1, f32[1,1024]{1,0:T(1,128)} %bitcast.1, ...), custom_call_target="tpu_custom_call" | custom-call | tf_op jit(solution)/shard_map/linear_attention/pallas_call | solution.py:383
  65.3 0.0 copy-start.2
  65.3 2.4 %copy.13 = bf16[512,1024]{1,0:T(8,128)(2,1)} copy(bf16[512,1024]{1,0:T(8,128)(2,1)} %get-tuple-element.8) | data formatting | bytes 2097152
  67.6 0.0 copy-done.2
  67.6 0.0 copy-start.1
  67.6 1.0 %copy.14 = bf16[512,1024]{1,0:T(8,128)(2,1)} copy(bf16[512,1024]{1,0:T(8,128)(2,1)S(1)} %copy-done.2) | data formatting | bytes 2097152
  68.6 0.6 copy-done.1
  69.2 0.0 copy-start
  69.2 1.0 %copy.15 = bf16[512,1024]{1,0:T(8,128)(2,1)} copy(bf16[512,1024]{1,0:T(8,128)(2,1)S(1)} %copy-done.1) | data formatting | bytes 2097152
  70.2 0.6 copy-done
  70.8 1.0 %copy.16 = bf16[512,1024]{1,0:T(8,128)(2,1)} copy(bf16[512,1024]{1,0:T(8,128)(2,1)S(1)} %copy-done) | data formatting | bytes 2097152
Async XLA Ops:
  65.3 2.4 %copy-start.2 = (bf16[512,1024]{1,0:T(8,128)(2,1)S(1)}, bf16[512,1024]{1,0:T(8,128)(2,1)}, u32[]{:S(2)}) copy-start(bf16[512,1024]{1,0:T(8,128)(2,1)} %get-tuple-element.9) | copy-start | bytes 3145732
  67.6 1.6 %copy-start.1 = (bf16[512,1024]{1,0:T(8,128)(2,1)S(1)}, bf16[512,1024]{1,0:T(8,128)(2,1)}, u32[]{:S(2)}) copy-start(bf16[512,1024]{1,0:T(8,128)(2,1)} %get-tuple-element.10) | copy-start | bytes 3145732
  69.2 1.6 %copy-start = (bf16[512,1024]{1,0:T(8,128)(2,1)S(1)}, bf16[512,1024]{1,0:T(8,128)(2,1)}, u32[]{:S(2)}) copy-start(bf16[512,1024]{1,0:T(8,128)(2,1)} %get-tuple-element.11) | copy-start | bytes 3145732

commit v2 on v1

--- a/solution.py
+++ b/solution.py
@@ -10,7 +10,8 @@
 HD = 128
 BLK = 512
 NY = 4
-CHUNKS = 2
+CHUNKS = 4
+LAST = 4
 HALF = BLK // 2
 F32 = jnp.float32
 BF16 = jnp.bfloat16
@@ -133,13 +134,28 @@
             copy.wait_send()
 
 
-def kernel(nz, nh, heads, q_hbm, k_hbm, v_hbm, gain_hbm, g_hbm, normed_hbm, qgrad_hbm, kgrad_hbm, vgrad_hbm,
-           q, k, v, gain, g, scores, att, dout, kpart, vpart, normed, qgrad, kgrad, vgrad, state_bf, squares,
+def lanes(h):
+    return pl.ds(pl.multiple_of(h * HD, HD), HD)
+
+
+def sub(h):
+    return pl.ds(pl.multiple_of(h * HD, HD), HD)
+
+
+def each(first, count, body):
+    def step(h, _):
+        body(h)
+        return 0
+
+    lax.fori_loop(first, first + count, step, 0)
+
+
+def kernel(nz, nh, heads, q_hbm, k_hbm, v_hbm, gain_hbm, g_hbm, normed, qgrad, kpart, vpart, later_bf, k, v,
+           q, gain, g, scores, att, dout, state_bf, squares,
            products, inv_b, coef_b, head_src, head_dst, *rest):
     fwd_refs, bwd_refs = rest[0:8], rest[8:16]
     fwd_sems, bwd_sems = rest[16:20], rest[20:24]
-    in_sem, out_sem, head_send, head_recv = rest[24:28]
-    later_bf = rest[28]
+    in_sem, head_send, head_recv = rest[24:27]
     scale = HD ** (-0.5)
     per = heads // CHUNKS
     rows = per * HD
@@ -174,19 +190,6 @@
 
     fwd = Scan(nz, rows, False, fwd_refs, fwd_sems)
     bwd = Scan(nz, rows, True, bwd_refs, bwd_sems)
-
-    def lanes(h):
-        return pl.ds(pl.multiple_of(h * HD, HD), HD)
-
-    def sub(h):
-        return pl.ds(pl.multiple_of(h * HD, HD), HD)
-
-    def each(first, count, body):
-        def step(h, _):
-            body(h)
-            return 0
-
-        lax.fori_loop(first, first + count, step, 0)
 
     def kv(h):
         fwd.block[sub(h), :] = dot_tn(k[:, lanes(h)], v[:, lanes(h)])
@@ -296,6 +299,30 @@
         vpart[:HALF, lanes(h)] = dot_tn(scores[h, 0], d[:HALF]) + dot_tn(scores[h, 1], d[HALF:])
         vpart[HALF:, lanes(h)] = dot_tn(scores[h, 2], d[HALF:])
 
+    each(0, heads // 2, back)
+    for c in range(CHUNKS):
+        moving[c] = bwd.z_out(c, moving[c])
+    each(heads // 2, heads - heads // 2, back)
+    for c in range(CHUNKS):
+        moving[c] = bwd.z_back(c, moving[c])
+    for c in range(CHUNKS):
+        moving[c] = bwd.y_back(c, moving[c])
+    for c in range(CHUNKS):
+        for copy in moving[c]:
+            copy.wait_recv()
+
+        later_bf[pl.ds(c * rows, rows), :] = bwd.b4[c].reshape(rows, HD).astype(BF16)
+
+    fwd.finish()
+    for copy in head_copies:
+        copy.wait_send()
+    bwd.finish()
+
+
+def finish_kernel(heads, normed, qgrad, kpart, vpart, later_bf, k, v, normed_hbm, qgrad_hbm, kgrad_hbm, vgrad_hbm,
+                  kgrad, vgrad, out_sem):
+    scale = HD ** (-0.5)
+    per = heads // LAST
     outs = []
 
     def put(src, dst):
@@ -303,35 +330,19 @@
         copy.start()
         outs.append(copy)
 
-    each(0, heads // 2, back)
-    for c in range(CHUNKS):
-        moving[c] = bwd.z_out(c, moving[c])
-    each(heads // 2, heads - heads // 2, back)
-    for c in range(CHUNKS):
-        moving[c] = bwd.z_back(c, moving[c])
     put(normed, normed_hbm)
     put(qgrad, qgrad_hbm)
-    for c in range(CHUNKS):
-        moving[c] = bwd.y_back(c, moving[c])
-    for c in range(CHUNKS):
-        for copy in moving[c]:
-            copy.wait_recv()
-
-        def last(h):
-            here = later_bf[sub(h), :]
-            kgrad[:, lanes(h)] = (scale * (kpart[:, lanes(h)] + dot_nt(v[:, lanes(h)], here))).astype(BF16)
-            vgrad[:, lanes(h)] = (vpart[:, lanes(h)] + scale * dot_nn(k[:, lanes(h)], here)).astype(BF16)
-
-        later_bf[pl.ds(c * rows, rows), :] = bwd.b4[c].reshape(rows, HD).astype(BF16)
+
+    def last(h):
+        here = later_bf[sub(h), :]
+        kgrad[:, lanes(h)] = (scale * (kpart[:, lanes(h)] + dot_nt(v[:, lanes(h)], here))).astype(BF16)
+        vgrad[:, lanes(h)] = (vpart[:, lanes(h)] + scale * dot_nn(k[:, lanes(h)], here)).astype(BF16)
+
+    for c in range(LAST):
         each(c * per, per, last)
-        cols = pl.ds(c * rows, rows)
+        cols = pl.ds(c * per * HD, per * HD)
         put(kgrad.at[:, cols], kgrad_hbm.at[:, cols])
         put(vgrad.at[:, cols], vgrad_hbm.at[:, cols])
-
-    fwd.finish()
-    for copy in head_copies:
-        copy.wait_send()
-    bwd.finish()
     for copy in outs:
         copy.wait()
 
@@ -365,32 +376,44 @@
 
     big_f32, big_bf16 = vmem((blk, width), F32), vmem((blk, width), BF16)
     scratch = [
-        big_bf16, big_bf16, big_bf16, vmem((1, width), F32), big_bf16,
+        big_bf16, vmem((1, width), F32), big_bf16,
         vmem((heads, 3, HALF, HALF), BF16),
-        big_f32, big_bf16, big_f32, big_f32,
-        big_bf16, big_bf16, big_bf16, big_bf16,
+        big_f32, big_bf16,
         vmem((heads * HD, HD), BF16),
         vmem((blk, HD), F32), vmem((blk, HD), F32), vmem((blk, HD), F32), vmem((blk, HD), F32),
         vmem((8, HD), F32), vmem((nh, 8, HD), F32),
         *scan_refs(), *scan_refs(), *scan_sems(), *scan_sems(),
         pltpu.SemaphoreType.DMA((2 * CHUNKS + 3,)),
-        pltpu.SemaphoreType.DMA((2 + 2 * CHUNKS,)),
         pltpu.SemaphoreType.DMA((nh - 1,)),
         pltpu.SemaphoreType.DMA((nh - 1,)),
-        vmem((heads * HD, HD), BF16),
     ]
     out = jax.ShapeDtypeStruct((blk, width), BF16)
-    return pl.pallas_call(
+    anywhere, in_vmem = pl.BlockSpec(memory_space=pl.ANY), pl.BlockSpec(memory_space=pltpu.VMEM)
+    parts = pl.pallas_call(
         functools.partial(kernel, nz, nh, heads),
-        out_shape=(out, out, out, out),
-        in_specs=[pl.BlockSpec(memory_space=pl.ANY)] * 5,
-        out_specs=(pl.BlockSpec(memory_space=pl.ANY),) * 4,
+        out_shape=(
+            big_bf16, big_bf16, big_f32, big_f32, vmem((heads * HD, HD), BF16), big_bf16, big_bf16,
+        ),
+        in_specs=[anywhere] * 5,
+        out_specs=(in_vmem,) * 7,
         scratch_shapes=scratch,
         compiler_params=pltpu.CompilerParams(
-            collective_id=0, has_side_effects=True, vmem_limit_bytes=56 * 1024 * 1024
+            collective_id=0, has_side_effects=True, vmem_limit_bytes=28 * 1024 * 1024
         ),
         name="linear_attention",
-    )(queries, keys, values, norm_gain.reshape(1, width), out_grad)
+    )(*[
+        pltpu.with_memory_space_constraint(a, pltpu.HBM)
+        for a in (queries, keys, values, norm_gain.reshape(1, width), out_grad)
+    ])
+    return pl.pallas_call(
+        functools.partial(finish_kernel, heads),
+        out_shape=(out,) * 4,
+        in_specs=[in_vmem] * 7,
+        out_specs=(anywhere,) * 4,
+        scratch_shapes=[big_bf16, big_bf16, pltpu.SemaphoreType.DMA((2 + 2 * LAST,))],
+        compiler_params=pltpu.CompilerParams(vmem_limit_bytes=28 * 1024 * 1024),
+        name="key_value_grads",
+    )(*parts)
 
 
 def solution(mesh):

time: 72 us -> 65.2 us (0.906)
  local copies, waits for them, and re-layouts: 6.53 us -> 0 us
    unnamed x10 -> x0, local copies, waits for them, and re-layouts: 6.53 us -> none
    pallas_call x1 -> x2, Pallas kernels: 64.6 us -> 64.5 us  [the longest x1 61.7 us: local(): pl.pallas_call(functools.partial(kernel, nz, nh, heads), out_shape=(big_b...]
where the time goes in v2:
time: 65.2 us; the launch traced here: 65.1 us
  Pallas kernels  64.5 us (99%)
    pallas_call x1, Pallas kernels, local(): pl.pallas_call(functools.partial(kernel, nz, nh, heads), out_shape=(big_b...  61.7 us
    pallas_call x1, Pallas kernels, local(): pl.pallas_call(functools.partial(finish_kernel, heads), out_shape=(out,)...  2.8 us

profile of v2, /device:TPU:8, one launch (start us, length us, event | category | flops | bytes accessed | tf_op | source)
XLA Modules:
  0.0 65.1 jit_solution(4163608583381241609)
XLA Ops:
  0.6 61.7 %linear_attention.1 = (bf16[512,1024]{1,0:T(8,128)(2,1)S(1)}, bf16[512,1024]{1,0:T(8,128)(2,1)S(1)}, f32[512,1024]{1,0:T(8,128)S(1)}, f32[512,1024]{1,0:T(8,128)...) custom-call(bf16[512,1024]{1,0:T(8,128)(2,1)} %q_hbm.1, ...), custom_call_target="tpu_custom_call" | custom-call | tf_op jit(solution)/shard_map/linear_attention/pallas_call | solution.py:392
  62.3 2.8 %key_value_grads.1 = (bf16[512,1024]{1,0:T(8,128)(2,1)}, bf16[512,1024]{1,0:T(8,128)(2,1)}, bf16[512,1024]{1,0:T(8,128)(2,1)}, bf16[512,1024]{1,0:T(8,128)(2,1)}) custom-call(bf16[512,1024]{1,0:T(8,128)(2,1)S(1)} %get-tuple-element.11.normed, bf16[512,1024]{1,0:T(8,128)(2,1)S(1)} %get-tuple-element.12.qgrad, f32[512,1024]{1,0:T(8,128)S(1)} %get-tuple-element.13.kpart, ...), custom_call_target="tpu_custom_call" | custom-call | tf_op jit(solution)/shard_map/key_value_grads/pallas_call | solution.py:408

commit v3 on v2

--- a/solution.py
+++ b/solution.py
@@ -11,12 +11,12 @@
 BLK = 512
 NY = 4
 CHUNKS = 4
-LAST = 4
+AHEAD = (3, 3)
+BEHIND = (2, 2, 2)
 HALF = BLK // 2
 F32 = jnp.float32
 BF16 = jnp.bfloat16
 MESH = pl.DeviceIdType.MESH
-EXACT = lax.Precision.HIGHEST
 
 
 def dot_nn(a, b):
@@ -31,12 +31,12 @@
     return lax.dot_general(a, b, (((0,), (0,)), ((), ())), preferred_element_type=F32)
 
 
-def exact_nt(a, b):
-    return lax.dot_general(a, b, (((1,), (1,)), ((), ())), precision=EXACT, preferred_element_type=F32)
-
-
-def exact_tn(a, b):
-    return lax.dot_general(a, b, (((0,), (0,)), ((), ())), precision=EXACT, preferred_element_type=F32)
+def split(a, count):
+    parts = []
+    for _ in range(count):
+        parts.append(a.astype(BF16))
+        a = a - parts[-1].astype(F32)
+    return parts
 
 
 class Scan:
@@ -150,8 +150,8 @@
     lax.fori_loop(first, first + count, step, 0)
 
 
-def kernel(nz, nh, heads, q_hbm, k_hbm, v_hbm, gain_hbm, g_hbm, normed, qgrad, kpart, vpart, later_bf, k, v,
-           q, gain, g, scores, att, dout, state_bf, squares,
+def kernel(nz, nh, heads, q_hbm, k_hbm, v_hbm, gain_hbm, g_hbm, normed, qgrad, kgrad, vgrad, kpart_end, vpart_end,
+           later_end, k_end, v_end, q, k, v, gain, g, grad_norm, scores, att, dout, kpart, vpart, state_bf, squares,
            products, inv_b, coef_b, head_src, head_dst, *rest):
     fwd_refs, bwd_refs = rest[0:8], rest[8:16]
     fwd_sems, bwd_sems = rest[16:20], rest[20:24]
@@ -162,16 +162,6 @@
     width = heads * HD
     seq, head = lax.axis_index("seq"), lax.axis_index("head")
     z, y = lax.div(seq, NY), lax.rem(seq, NY)
-
-    barrier = pltpu.get_barrier_semaphore()
-    for d in range(1, NY):
-        to = z * NY + lax.rem(y + d, NY)
-        pl.semaphore_signal(barrier, inc=1, device_id=(to, head), device_id_type=MESH)
-    for d in range(1, nz):
-        to = lax.rem(z + d, nz) * NY + y
-        pl.semaphore_signal(barrier, inc=1, device_id=(to, head), device_id_type=MESH)
-    for d in range(1, nh):
-        pl.semaphore_signal(barrier, inc=1, device_id=(seq, lax.rem(head + d, nh)), device_id_type=MESH)
 
     loads = []
     for c in range(CHUNKS):
@@ -188,6 +178,16 @@
         copy.start()
         late.append(copy)
 
+    barrier = pltpu.get_barrier_semaphore()
+    for d in range(1, NY):
+        to = z * NY + lax.rem(y + d, NY)
+        pl.semaphore_signal(barrier, inc=1, device_id=(to, head), device_id_type=MESH)
+    for d in range(1, nz):
+        to = lax.rem(z + d, nz) * NY + y
+        pl.semaphore_signal(barrier, inc=1, device_id=(to, head), device_id_type=MESH)
+    for d in range(1, nh):
+        pl.semaphore_signal(barrier, inc=1, device_id=(seq, lax.rem(head + d, nh)), device_id_type=MESH)
+
     fwd = Scan(nz, rows, False, fwd_refs, fwd_sems)
     bwd = Scan(nz, rows, True, bwd_refs, bwd_sems)
 
@@ -198,7 +198,8 @@
     for c in range(CHUNKS):
         for copy in loads[c]:
             copy.wait()
-        each(c * per, per, kv)
+        for h in range(c * per, (c + 1) * per):
+            kv(h)
         if c == 0:
             pl.semaphore_wait(barrier, (NY - 1) + (nz - 1) + (nh - 1))
         moving.append(fwd.y_out(c))
@@ -219,38 +220,41 @@
         scores[h, 0], scores[h, 1], scores[h, 2] = top, low, end
         att[:HALF, lanes(h)] = dot_nn(top, vh[:HALF])
         att[HALF:, lanes(h)] = dot_nn(low, vh[:HALF]) + dot_nn(end, vh[HALF:])
-
-    each(0, heads // 2, intra)
+        grad_norm[:, lanes(h)] = g[:, lanes(h)].astype(F32) * gain[:, lanes(h)]
+
+    each(0, AHEAD[0], intra)
     for c in range(CHUNKS):
         moving[c] = fwd.z_out(c, moving[c])
-    each(heads // 2, heads - heads // 2, intra)
+    each(AHEAD[0], AHEAD[1], intra)
     for c in range(CHUNKS):
         moving[c] = fwd.z_back(c, moving[c])
-    squares[...] = jnp.zeros_like(squares)
-    products[...] = jnp.zeros_like(products)
+    each(AHEAD[0] + AHEAD[1], heads - AHEAD[0] - AHEAD[1], intra)
     for c in range(CHUNKS):
         moving[c] = fwd.y_back(c, moving[c])
-
     for c in range(CHUNKS):
         for copy in moving[c]:
             copy.wait_recv()
-        state_bf[pl.ds(c * rows, rows), :] = fwd.b4[c].reshape(rows, HD).astype(BF16)
-
-        def attend(h):
-            a = att[:, lanes(h)] + scale * dot_nn(q[:, lanes(h)], state_bf[sub(h), :])
+        here = fwd.b4[c].reshape(rows, HD).astype(BF16)
+        state_bf[pl.ds(c * rows, rows), :] = here
+        sq, pr = (squares[...], products[...]) if c > 0 else (0.0, 0.0)
+        for i in range(per):
+            h = c * per + i
+            a = att[:, lanes(h)] + scale * dot_nn(q[:, lanes(h)], here[i * HD : (i + 1) * HD])
             att[:, lanes(h)] = a
-            squares[...] += a * a
-            products[...] += a * (g[:, lanes(h)].astype(F32) * gain[:, lanes(h)])
-
-        each(c * per, per, attend)
+            sq = sq + a * a
+            pr = pr + a * grad_norm[:, lanes(h)]
+        squares[...], products[...] = sq, pr
 
     row = lax.broadcasted_iota(jnp.int32, (8, HD), 0)
     groups = BLK // HD
     packed = jnp.zeros((8, HD), F32)
     for t in range(groups):
         part = pl.ds(t * HD, HD)
-        packed = packed + exact_nt((row == t).astype(F32), squares[part, :])
-        packed = packed + exact_nt((row == groups + t).astype(F32), products[part, :])
+        for first, totals in ((0, squares), (groups, products)):
+            pick = (row == first + t).astype(BF16)
+            packed = packed + dot_nt(
+                jnp.concatenate([pick, pick], axis=1), jnp.concatenate(split(totals[part, :], 2), axis=1)
+            )
     head_src[...] = packed
     head_copies = []
     for d in range(1, nh):
@@ -269,20 +273,21 @@
     full = nh * width
     inv = 1.0 / jnp.sqrt(sums[:groups] / full + 1e-06)
     proj = (sums[groups:] * inv) / full
-    both = jnp.concatenate([inv, (inv * proj) * inv], axis=0)
+    both = jnp.concatenate(split(jnp.concatenate([inv, (inv * proj) * inv], axis=0), 3), axis=0)
     for t in range(groups):
         part = pl.ds(t * HD, HD)
-        inv_b[part, :] = exact_tn(both, (row == t).astype(F32))
-        coef_b[part, :] = exact_tn(both, (row == groups + t).astype(F32))
+        for first, spread in ((0, inv_b), (groups, coef_b)):
+            pick = (row == first + t).astype(BF16)
+            spread[part, :] = dot_tn(both, jnp.concatenate([pick, pick, pick], axis=0))
 
     def grad(h):
-        gn = g[:, lanes(h)].astype(F32) * gain[:, lanes(h)]
-        d = (gn * inv_b[...] - att[:, lanes(h)] * coef_b[...]).astype(BF16)
+        d = (grad_norm[:, lanes(h)] * inv_b[...] - att[:, lanes(h)] * coef_b[...]).astype(BF16)
         dout[:, lanes(h)] = d
         bwd.block[sub(h), :] = dot_tn(q[:, lanes(h)], d)
 
     for c in range(CHUNKS):
-        each(c * per, per, grad)
+        for h in range(c * per, (c + 1) * per):
+            grad(h)
         moving[c] = bwd.y_out(c)
 
     def back(h):
@@ -299,19 +304,35 @@
         vpart[:HALF, lanes(h)] = dot_tn(scores[h, 0], d[:HALF]) + dot_tn(scores[h, 1], d[HALF:])
         vpart[HALF:, lanes(h)] = dot_tn(scores[h, 2], d[HALF:])
 
-    each(0, heads // 2, back)
+    done = 0
+    each(done, BEHIND[0], back)
+    done += BEHIND[0]
     for c in range(CHUNKS):
         moving[c] = bwd.z_out(c, moving[c])
-    each(heads // 2, heads - heads // 2, back)
+    each(done, BEHIND[1], back)
+    done += BEHIND[1]
     for c in range(CHUNKS):
         moving[c] = bwd.z_back(c, moving[c])
+    each(done, BEHIND[2], back)
+    done += BEHIND[2]
     for c in range(CHUNKS):
         moving[c] = bwd.y_back(c, moving[c])
+    each(done, heads - done, back)
+    end = pl.ds((CHUNKS - 1) * rows, rows)
+    k_end[...], v_end[...] = k[:, end], v[:, end]
+    kpart_end[...], vpart_end[...] = kpart[:, end], vpart[:, end]
     for c in range(CHUNKS):
         for copy in moving[c]:
             copy.wait_recv()
-
-        later_bf[pl.ds(c * rows, rows), :] = bwd.b4[c].reshape(rows, HD).astype(BF16)
+        here = bwd.b4[c].reshape(rows, HD).astype(BF16)
+        if c == CHUNKS - 1:
+            later_end[...] = here
+            break
+        for i in range(per):
+            h = c * per + i
+            one = here[i * HD : (i + 1) * HD]
+            kgrad[:, lanes(h)] = (scale * (kpart[:, lanes(h)] + dot_nt(v[:, lanes(h)], one))).astype(BF16)
+            vgrad[:, lanes(h)] = (vpart[:, lanes(h)] + scale * dot_nn(k[:, lanes(h)], one)).astype(BF16)
 
     fwd.finish()
     for copy in head_copies:
@@ -319,10 +340,9 @@
     bwd.finish()
 
 
-def finish_kernel(heads, normed, qgrad, kpart, vpart, later_bf, k, v, normed_hbm, qgrad_hbm, kgrad_hbm, vgrad_hbm,
-                  kgrad, vgrad, out_sem):
+def finish_kernel(per, normed, qgrad, kgrad, vgrad, kpart, vpart, later, k, v, normed_hbm, qgrad_hbm, kgrad_hbm,
+                  vgrad_hbm, kgrad_end, vgrad_end, out_sem):
     scale = HD ** (-0.5)
-    per = heads // LAST
     outs = []
 
     def put(src, dst):
@@ -330,19 +350,16 @@
         copy.start()
         outs.append(copy)
 
+    begun = kgrad.shape[1] - per * HD
+    for src, dst in ((kgrad, kgrad_hbm), (vgrad, vgrad_hbm)):
+        put(src.at[:, pl.ds(0, begun)], dst.at[:, pl.ds(0, begun)])
     put(normed, normed_hbm)
     put(qgrad, qgrad_hbm)
-
-    def last(h):
-        here = later_bf[sub(h), :]
-        kgrad[:, lanes(h)] = (scale * (kpart[:, lanes(h)] + dot_nt(v[:, lanes(h)], here))).astype(BF16)
-        vgrad[:, lanes(h)] = (vpart[:, lanes(h)] + scale * dot_nn(k[:, lanes(h)], here)).astype(BF16)
-
-    for c in range(LAST):
-        each(c * per, per, last)
-        cols = pl.ds(c * per * HD, per * HD)
-        put(kgrad.at[:, cols], kgrad_hbm.at[:, cols])
-        put(vgrad.at[:, cols], vgrad_hbm.at[:, cols])
+    for h in range(per):
+        kgrad_end[:, lanes(h)] = (scale * (kpart[:, lanes(h)] + dot_nt(v[:, lanes(h)], later[sub(h), :]))).astype(BF16)
+        vgrad_end[:, lanes(h)] = (vpart[:, lanes(h)] + scale * dot_nn(k[:, lanes(h)], later[sub(h), :])).astype(BF16)
+    for src, dst in ((kgrad_end, kgrad_hbm), (vgrad_end, vgrad_hbm)):
+        put(src, dst.at[:, pl.ds(begun, per * HD)])
     for copy in outs:
         copy.wait()
 
@@ -375,10 +392,11 @@
         return [dma((y,)), dma((y,)), dma((zz,)), dma((zz,))]
 
     big_f32, big_bf16 = vmem((blk, width), F32), vmem((blk, width), BF16)
+    end_f32, end_bf16 = vmem((blk, rows), F32), vmem((blk, rows), BF16)
     scratch = [
-        big_bf16, vmem((1, width), F32), big_bf16,
+        big_bf16, big_bf16, big_bf16, vmem((1, width), F32), big_bf16, big_f32,
         vmem((heads, 3, HALF, HALF), BF16),
-        big_f32, big_bf16,
+        big_f32, big_bf16, big_f32, big_f32,
         vmem((heads * HD, HD), BF16),
         vmem((blk, HD), F32), vmem((blk, HD), F32), vmem((blk, HD), F32), vmem((blk, HD), F32),
         vmem((8, HD), F32), vmem((nh, 8, HD), F32),
@@ -392,13 +410,13 @@
     parts = pl.pallas_call(
         functools.partial(kernel, nz, nh, heads),
         out_shape=(
-            big_bf16, big_bf16, big_f32, big_f32, vmem((heads * HD, HD), BF16), big_bf16, big_bf16,
+            big_bf16, big_bf16, big_bf16, big_bf16, end_f32, end_f32, vmem((rows, HD), BF16), end_bf16, end_bf16,
         ),
         in_specs=[anywhere] * 5,
-        out_specs=(in_vmem,) * 7,
+        out_specs=(in_vmem,) * 9,
         scratch_shapes=scratch,
         compiler_params=pltpu.CompilerParams(
-            collective_id=0, has_side_effects=True, vmem_limit_bytes=28 * 1024 * 1024
+            collective_id=0, has_side_effects=True, vmem_limit_bytes=40 * 1024 * 1024
         ),
         name="linear_attention",
     )(*[
@@ -406,11 +424,11 @@
         for a in (queries, keys, values, norm_gain.reshape(1, width), out_grad)
     ])
     return pl.pallas_call(
-        functools.partial(finish_kernel, heads),
+        functools.partial(finish_kernel, heads // CHUNKS),
         out_shape=(out,) * 4,
-        in_specs=[in_vmem] * 7,
+        in_specs=[in_vmem] * 9,
         out_specs=(anywhere,) * 4,
-        scratch_shapes=[big_bf16, big_bf16, pltpu.SemaphoreType.DMA((2 + 2 * LAST,))],
+        scratch_shapes=[end_bf16, end_bf16, pltpu.SemaphoreType.DMA((6,))],
         compiler_params=pltpu.CompilerParams(vmem_limit_bytes=28 * 1024 * 1024),
         name="key_value_grads",
     )(*parts)

time: 65.2 us -> 61.4 us (0.942)
  Pallas kernels: 64.5 us -> 60.7 us
    pallas_call x1, Pallas kernels: 61.7 us -> 58.6 us  [local(): pl.pallas_call(functools.partial(kernel, nz, nh, heads), out_shape=(big_b...]
    pallas_call x1, Pallas kernels: 2.8 us -> 2.07 us  [local(): pl.pallas_call(functools.partial(finish_kernel, heads // CHUNKS), out_sha...]
where the time goes in v3:
time: 61.4 us; the launch traced here: 61.3 us
  Pallas kernels  60.7 us (99%)
  between operations  0.64 us (1%)
    pallas_call x1, Pallas kernels, local(): pl.pallas_call(functools.partial(kernel, nz, nh, heads), out_shape=(big_b...  58.6 us
    pallas_call x1, Pallas kernels, local(): pl.pallas_call(functools.partial(finish_kernel, heads // CHUNKS), out_sha...  2.07 us

profile of v3, /device:TPU:8, one launch (start us, length us, event | category | flops | bytes accessed | tf_op | source)
XLA Modules:
  0.0 61.3 jit_solution(9291565950287309674)
XLA Ops:
  0.6 58.6 %linear_attention.1 = (bf16[512,1024]{1,0:T(8,128)(2,1)S(1)}, bf16[512,1024]{1,0:T(8,128)(2,1)S(1)}, bf16[512,1024]{1,0:T(8,128)(2,1)S(1)}, bf16[512,1024]{1,0:T...) custom-call(bf16[512,1024]{1,0:T(8,128)(2,1)} %q_hbm.1, ...), custom_call_target="tpu_custom_call" | custom-call | tf_op jit(solution)/shard_map/linear_attention/pallas_call | solution.py:410
  59.2 2.1 %key_value_grads.1 = (bf16[512,1024]{1,0:T(8,128)(2,1)}, bf16[512,1024]{1,0:T(8,128)(2,1)}, bf16[512,1024]{1,0:T(8,128)(2,1)}, bf16[512,1024]{1,0:T(8,128)(2,1)}) custom-call(bf16[512,1024]{1,0:T(8,128)(2,1)S(1)} %get-tuple-element.13.normed, bf16[512,1024]{1,0:T(8,128)(2,1)S(1)} %get-tuple-element.14.qgrad, bf16[512,1024]{1,0:T(8,128)(2,1)S(1)} %get-tuple-element.15.kgrad, ...), custom_call_target="tpu_custom_call" | custom-call | tf_op jit(solution)/shard_map/key_value_grads/pallas_call | solution.py:426

commit v4 on v3

--- a/solution.py
+++ b/solution.py
@@ -11,6 +11,8 @@
 BLK = 512
 NY = 4
 CHUNKS = 4
+ORDER = (1, 2, 0, 3)
+ARRIVAL = (1, 2, 0, 3)
 AHEAD = (3, 3)
 BEHIND = (2, 2, 2)
 HALF = BLK // 2
@@ -39,10 +41,15 @@
     return parts
 
 
+def far_first(count):
+    return sorted(range(1, count), key=lambda d: -min(d, count - d))
+
+
 class Scan:
     def __init__(self, nz, rows, reverse, refs, sems):
         self.nz, self.rows, self.reverse = nz, rows, reverse
-        self.block, self.b1, self.tot, self.b2, self.pre, self.b3, self.ret, self.b4 = refs
+        self.block, self.b1, self.tot, self.b2, self.pre, self.b3, self.ret, self.b4 = refs[:8]
+        self.a1, self.a2, self.a3, self.a4, self.a5 = refs[8:]
         self.ysend, self.yrecv, self.zsend, self.zrecv = sems
         seq = lax.axis_index("seq")
         self.head = lax.axis_index("head")
@@ -93,9 +100,8 @@
         def part(j):
             return self.tot.at[c, pl.ds(pl.multiple_of(j * self.piece, 8), self.piece)]
 
-        far = sorted(range(1, self.nz), key=lambda d: -min(d, self.nz - d))
-        copies = self.begin([
-            self.z_copy(0, c, d, part(lax.rem(self.z + d, self.nz)), self.b2.at[c, self.z]) for d in far
+        copies = self.begin([
+            self.z_copy(0, c, d, part(lax.rem(self.z + d, self.nz)), self.b2.at[c, self.z]) for d in far_first(self.nz)
         ])
         self.b2[c, self.z] = part(self.z)[...]
         return copies
@@ -108,9 +114,8 @@
         for j in reversed(order) if self.reverse else order:
             self.pre[c, j] = total
             total = total + self.b2[c, j]
-        far = sorted(range(1, self.nz), key=lambda d: -min(d, self.nz - d))
-        copies = self.begin([
-            self.z_copy(1, c, d, self.pre.at[c, lax.rem(self.z + d, self.nz)], self.b3.at[c, self.z]) for d in far
+        copies = self.begin([
+            self.z_copy(1, c, d, self.pre.at[c, lax.rem(self.z + d, self.nz)], self.b3.at[c, self.z]) for d in far_first(self.nz)
         ])
         self.b3[c, self.z] = self.pre[c, self.z]
         return copies
@@ -129,6 +134,76 @@
         self.b4[c, self.y] = self.ret[c, self.y]
         return copies
 
+    def a_out(self):
+        height = self.rows // self.nz
+
+        def part(j):
+            return self.block.at[pl.ds(pl.multiple_of(j * height, 8), height)]
+
+        copies = self.begin([
+            self.z_copy(0, 0, d, part(lax.rem(self.z + d, self.nz)), self.a1.at[self.z]) for d in far_first(self.nz)
+        ])
+        self.a1[self.z] = part(self.z)[...]
+        return copies
+
+    def a_mid(self, arriving):
+        for copy in arriving:
+            copy.wait_recv()
+        height = self.rows // self.nz // NY
+
+        def part(q):
+            return self.a1.at[:, pl.ds(pl.multiple_of(q * height, 8), height)]
+
+        copies = self.begin([
+            self.y_copy(0, 0, d, part(lax.rem(self.y + d, NY)), self.a2.at[self.y]) for d in (2, 1, 3)
+        ])
+        self.a2[self.y] = part(self.y)[...]
+        return copies
+
+    def a_back(self, arriving):
+        for copy in arriving:
+            copy.wait_recv()
+        order = [(j, i) for j in range(self.nz) for i in range(NY)]
+        total = jnp.zeros(self.a2.shape[2:], F32)
+        for j, i in reversed(order) if self.reverse else order:
+            self.a3[i, j] = total
+            total = total + self.a2[i, j]
+        copies = self.begin([
+            self.y_copy(1, 0, d, self.a3.at[lax.rem(self.y + d, NY)], self.a4.at[self.y]) for d in (2, 1, 3)
+        ])
+        self.a4[self.y] = self.a3[self.y]
+        return copies
+
+    def a_end(self, arriving):
+        for copy in arriving:
+            copy.wait_recv()
+        copies = self.begin([
+            self.z_copy(1, 0, d, self.a4.at[:, lax.rem(self.z + d, self.nz)], self.a5.at[self.z])
+            for d in far_first(self.nz)
+        ])
+        self.a5[self.z] = self.a4[:, self.z]
+        return copies
+
+    def first(self, c):
+        return self.a_out() if c == 0 else self.y_out(c)
+
+    def second(self, moving):
+        for c in ORDER:
+            moving[c] = self.a_mid(moving[c]) if c == 0 else self.z_out(c, moving[c])
+
+    def third(self, moving):
+        for c in ORDER:
+            moving[c] = self.a_back(moving[c]) if c == 0 else self.z_back(c, moving[c])
+
+    def fourth(self, moving):
+        for c in ORDER:
+            moving[c] = self.a_end(moving[c]) if c == 0 else self.y_back(c, moving[c])
+
+    def result(self, c, arriving):
+        for copy in arriving:
+            copy.wait_recv()
+        return (self.a5[...] if c == 0 else self.b4[c]).reshape(self.rows, HD).astype(BF16)
+
     def finish(self):
         for copy in self.sends:
             copy.wait_send()
@@ -153,9 +228,9 @@
 def kernel(nz, nh, heads, q_hbm, k_hbm, v_hbm, gain_hbm, g_hbm, normed, qgrad, kgrad, vgrad, kpart_end, vpart_end,
            later_end, k_end, v_end, q, k, v, gain, g, grad_norm, scores, att, dout, kpart, vpart, state_bf, squares,
            products, inv_b, coef_b, head_src, head_dst, *rest):
-    fwd_refs, bwd_refs = rest[0:8], rest[8:16]
-    fwd_sems, bwd_sems = rest[16:20], rest[20:24]
-    in_sem, head_send, head_recv = rest[24:27]
+    fwd_refs, bwd_refs = rest[0:13], rest[13:26]
+    fwd_sems, bwd_sems = rest[26:30], rest[30:34]
+    in_sem, head_send, head_recv = rest[34:37]
     scale = HD ** (-0.5)
     per = heads // CHUNKS
     rows = per * HD
@@ -164,7 +239,8 @@
     z, y = lax.div(seq, NY), lax.rem(seq, NY)
 
     loads = []
-    for c in range(CHUNKS):
+
+    def load(c):
         cols = pl.ds(c * rows, rows)
         pair = []
         for i, (src, dst) in enumerate(((k_hbm, k), (v_hbm, v))):
@@ -172,21 +248,25 @@
             copy.start()
             pair.append(copy)
         loads.append(pair)
+
+    load(0)
+    barrier = pltpu.get_barrier_semaphore()
+    for d in far_first(nz):
+        to = lax.rem(z + d, nz) * NY + y
+        pl.semaphore_signal(barrier, inc=1, device_id=(to, head), device_id_type=MESH)
+    for d in range(1, nh):
+        pl.semaphore_signal(barrier, inc=1, device_id=(seq, lax.rem(head + d, nh)), device_id_type=MESH)
+    for d in far_first(NY):
+        to = z * NY + lax.rem(y + d, NY)
+        pl.semaphore_signal(barrier, inc=1, device_id=(to, head), device_id_type=MESH)
+
+    for c in range(1, CHUNKS):
+        load(c)
     late = []
     for i, (src, dst) in enumerate(((q_hbm, q), (g_hbm, g), (gain_hbm, gain))):
         copy = pltpu.make_async_copy(src, dst, in_sem.at[2 * CHUNKS + i])
         copy.start()
         late.append(copy)
-
-    barrier = pltpu.get_barrier_semaphore()
-    for d in range(1, NY):
-        to = z * NY + lax.rem(y + d, NY)
-        pl.semaphore_signal(barrier, inc=1, device_id=(to, head), device_id_type=MESH)
-    for d in range(1, nz):
-        to = lax.rem(z + d, nz) * NY + y
-        pl.semaphore_signal(barrier, inc=1, device_id=(to, head), device_id_type=MESH)
-    for d in range(1, nh):
-        pl.semaphore_signal(barrier, inc=1, device_id=(seq, lax.rem(head + d, nh)), device_id_type=MESH)
 
     fwd = Scan(nz, rows, False, fwd_refs, fwd_sems)
     bwd = Scan(nz, rows, True, bwd_refs, bwd_sems)
@@ -202,7 +282,7 @@
             kv(h)
         if c == 0:
             pl.semaphore_wait(barrier, (NY - 1) + (nz - 1) + (nh - 1))
-        moving.append(fwd.y_out(c))
+        moving.append(fwd.first(c))
     for copy in late:
         copy.wait()
 
@@ -223,20 +303,15 @@
         grad_norm[:, lanes(h)] = g[:, lanes(h)].astype(F32) * gain[:, lanes(h)]
 
     each(0, AHEAD[0], intra)
-    for c in range(CHUNKS):
-        moving[c] = fwd.z_out(c, moving[c])
+    fwd.second(moving)
     each(AHEAD[0], AHEAD[1], intra)
-    for c in range(CHUNKS):
-        moving[c] = fwd.z_back(c, moving[c])
+    fwd.third(moving)
     each(AHEAD[0] + AHEAD[1], heads - AHEAD[0] - AHEAD[1], intra)
-    for c in range(CHUNKS):
-        moving[c] = fwd.y_back(c, moving[c])
-    for c in range(CHUNKS):
-        for copy in moving[c]:
-            copy.wait_recv()
-        here = fwd.b4[c].reshape(rows, HD).astype(BF16)
+    fwd.fourth(moving)
+    for c in ARRIVAL:
+        here = fwd.result(c, moving[c])
         state_bf[pl.ds(c * rows, rows), :] = here
-        sq, pr = (squares[...], products[...]) if c > 0 else (0.0, 0.0)
+        sq, pr = (0.0, 0.0) if c == ARRIVAL[0] else (squares[...], products[...])
         for i in range(per):
             h = c * per + i
             a = att[:, lanes(h)] + scale * dot_nn(q[:, lanes(h)], here[i * HD : (i + 1) * HD])
@@ -288,7 +363,7 @@
     for c in range(CHUNKS):
         for h in range(c * per, (c + 1) * per):
             grad(h)
-        moving[c] = bwd.y_out(c)
+        moving[c] = bwd.first(c)
 
     def back(h):
         qh, kh, vh, d = q[:, lanes(h)], k[:, lanes(h)], v[:, lanes(h)], dout[:, lanes(h)]
@@ -307,24 +382,19 @@
     done = 0
     each(done, BEHIND[0], back)
     done += BEHIND[0]
-    for c in range(CHUNKS):
-        moving[c] = bwd.z_out(c, moving[c])
+    bwd.second(moving)
     each(done, BEHIND[1], back)
     done += BEHIND[1]
-    for c in range(CHUNKS):
-        moving[c] = bwd.z_back(c, moving[c])
+    bwd.third(moving)
     each(done, BEHIND[2], back)
     done += BEHIND[2]
-    for c in range(CHUNKS):
-        moving[c] = bwd.y_back(c, moving[c])
+    bwd.fourth(moving)
     each(done, heads - done, back)
     end = pl.ds((CHUNKS - 1) * rows, rows)
     k_end[...], v_end[...] = k[:, end], v[:, end]
     kpart_end[...], vpart_end[...] = kpart[:, end], vpart[:, end]
-    for c in range(CHUNKS):
-        for copy in moving[c]:
-            copy.wait_recv()
-        here = bwd.b4[c].reshape(rows, HD).astype(BF16)
+    for c in ARRIVAL:
+        here = bwd.result(c, moving[c])
         if c == CHUNKS - 1:
             later_end[...] = here
             break
@@ -384,6 +454,11 @@
             vmem((CHUNKS, nz, piece, HD), F32),
             vmem((CHUNKS, NY, quarter, HD), F32),
             vmem((CHUNKS, NY, quarter, HD), F32),
+            vmem((nz, rows // nz, HD), F32),
+            vmem((NY, nz, rows // nz // NY, HD), F32),
+            vmem((NY, nz, rows // nz // NY, HD), F32),
+            vmem((NY, nz, rows // nz // NY, HD), F32),
+            vmem((nz, NY, rows // nz // NY, HD), F32),
         ]
 
     def scan_sems():

time: 61.4 us -> 60.7 us (0.989)
  Pallas kernels: 60.7 us -> 59.4 us
    pallas_call x1, Pallas kernels: 58.6 us -> 57.4 us  [local(): pl.pallas_call(functools.partial(kernel, nz, nh, heads), out_shape=(big_b...]
where the time goes in v4:
time: 60.7 us; the launch traced here: 60.1 us
  Pallas kernels  59.4 us (98%)
  between operations  0.64 us (1%)
    pallas_call x1, Pallas kernels, local(): pl.pallas_call(functools.partial(kernel, nz, nh, heads), out_shape=(big_b...  57.4 us
    pallas_call x1, Pallas kernels, local(): pl.pallas_call(functools.partial(finish_kernel, heads // CHUNKS), out_sha...  2.07 us

profile of v4, /device:TPU:8, one launch (start us, length us, event | category | flops | bytes accessed | tf_op | source)
XLA Modules:
  0.0 60.1 jit_solution(10012207293777021666)
XLA Ops:
  0.6 57.4 %linear_attention.1 = (bf16[512,1024]{1,0:T(8,128)(2,1)S(1)}, bf16[512,1024]{1,0:T(8,128)(2,1)S(1)}, bf16[512,1024]{1,0:T(8,128)(2,1)S(1)}, bf16[512,1024]{1,0:T...) custom-call(bf16[512,1024]{1,0:T(8,128)(2,1)} %q_hbm.1, ...), custom_call_target="tpu_custom_call" | custom-call | tf_op jit(solution)/shard_map/linear_attention/pallas_call | solution.py:485
  58.0 2.1 %key_value_grads.1 = (bf16[512,1024]{1,0:T(8,128)(2,1)}, bf16[512,1024]{1,0:T(8,128)(2,1)}, bf16[512,1024]{1,0:T(8,128)(2,1)}, bf16[512,1024]{1,0:T(8,128)(2,1)}) custom-call(bf16[512,1024]{1,0:T(8,128)(2,1)S(1)} %get-tuple-element.13.normed, bf16[512,1024]{1,0:T(8,128)(2,1)S(1)} %get-tuple-element.14.qgrad, bf16[512,1024]{1,0:T(8,128)(2,1)S(1)} %get-tuple-element.15.kgrad, ...), custom_call_target="tpu_custom_call" | custom-call | tf_op jit(solution)/shard_map/key_value_grads/pallas_call | solution.py:501

commit v5 on v4

--- a/solution.py
+++ b/solution.py
@@ -188,15 +188,15 @@
         return self.a_out() if c == 0 else self.y_out(c)
 
     def second(self, moving):
-        for c in ORDER:
+        for c in (1, 2, 0, 3):
             moving[c] = self.a_mid(moving[c]) if c == 0 else self.z_out(c, moving[c])
 
     def third(self, moving):
-        for c in ORDER:
+        for c in (1, 0, 2, 3):
             moving[c] = self.a_back(moving[c]) if c == 0 else self.z_back(c, moving[c])
 
     def fourth(self, moving):
-        for c in ORDER:
+        for c in (0, 1, 2, 3):
             moving[c] = self.a_end(moving[c]) if c == 0 else self.y_back(c, moving[c])
 
     def result(self, c, arriving):
@@ -388,8 +388,12 @@
     bwd.third(moving)
     each(done, BEHIND[2], back)
     done += BEHIND[2]
+    early, bwd.sends = bwd.sends, []
     bwd.fourth(moving)
     each(done, heads - done, back)
+    fwd.finish()
+    for copy in head_copies + early:
+        copy.wait_send()
     end = pl.ds((CHUNKS - 1) * rows, rows)
     k_end[...], v_end[...] = k[:, end], v[:, end]
     kpart_end[...], vpart_end[...] = kpart[:, end], vpart[:, end]
@@ -404,9 +408,6 @@
             kgrad[:, lanes(h)] = (scale * (kpart[:, lanes(h)] + dot_nt(v[:, lanes(h)], one))).astype(BF16)
             vgrad[:, lanes(h)] = (vpart[:, lanes(h)] + scale * dot_nn(k[:, lanes(h)], one)).astype(BF16)
 
-    fwd.finish()
-    for copy in head_copies:
-        copy.wait_send()
     bwd.finish()
 
 

time: 60.7 us -> 59.8 us (0.985)
  Pallas kernels: 59.4 us -> 58.7 us
    pallas_call x1, Pallas kernels: 57.4 us -> 56.6 us  [local(): pl.pallas_call(functools.partial(kernel, nz, nh, heads), out_shape=(big_b...]
where the time goes in v5:
time: 59.8 us; the launch traced here: 59.4 us
  Pallas kernels  58.7 us (98%)
  between operations  0.64 us (1%)
    pallas_call x1, Pallas kernels, local(): pl.pallas_call(functools.partial(kernel, nz, nh, heads), out_shape=(big_b...  56.6 us
    pallas_call x1, Pallas kernels, local(): pl.pallas_call(functools.partial(finish_kernel, heads // CHUNKS), out_sha...  2.07 us

profile of v5, /device:TPU:8, one launch (start us, length us, event | category | flops | bytes accessed | tf_op | source)
XLA Modules:
  0.0 59.4 jit_solution(7396327220633363729)
XLA Ops:
  0.6 56.6 %linear_attention.1 = (bf16[512,1024]{1,0:T(8,128)(2,1)S(1)}, bf16[512,1024]{1,0:T(8,128)(2,1)S(1)}, bf16[512,1024]{1,0:T(8,128)(2,1)S(1)}, bf16[512,1024]{1,0:T...) custom-call(bf16[512,1024]{1,0:T(8,128)(2,1)} %q_hbm.1, ...), custom_call_target="tpu_custom_call" | custom-call | tf_op jit(solution)/shard_map/linear_attention/pallas_call | solution.py:486
  57.3 2.1 %key_value_grads.1 = (bf16[512,1024]{1,0:T(8,128)(2,1)}, bf16[512,1024]{1,0:T(8,128)(2,1)}, bf16[512,1024]{1,0:T(8,128)(2,1)}, bf16[512,1024]{1,0:T(8,128)(2,1)}) custom-call(bf16[512,1024]{1,0:T(8,128)(2,1)S(1)} %get-tuple-element.13.normed, bf16[512,1024]{1,0:T(8,128)(2,1)S(1)} %get-tuple-element.14.qgrad, bf16[512,1024]{1,0:T(8,128)(2,1)S(1)} %get-tuple-element.15.kgrad, ...), custom_call_target="tpu_custom_call" | custom-call | tf_op jit(solution)/shard_map/key_value_grads/pallas_call | solution.py:502

commit v6 on v5

--- a/solution.py
+++ b/solution.py
@@ -192,7 +192,7 @@
             moving[c] = self.a_mid(moving[c]) if c == 0 else self.z_out(c, moving[c])
 
     def third(self, moving):
-        for c in (1, 0, 2, 3):
+        for c in (0, 1, 2, 3):
             moving[c] = self.a_back(moving[c]) if c == 0 else self.z_back(c, moving[c])
 
     def fourth(self, moving):
@@ -332,7 +332,7 @@
             )
     head_src[...] = packed
     head_copies = []
-    for d in range(1, nh):
+    for d in far_first(nh):
         copy = pltpu.make_async_remote_copy(
             src_ref=head_src, dst_ref=head_dst.at[head], send_sem=head_send.at[d - 1], recv_sem=head_recv.at[d - 1],
             device_id=(seq, lax.rem(head + d, nh)), device_id_type=MESH,

time: 59.8 us -> 59.5 us (level)
  no operation moved by 1% of the time
where the time goes in v6:
time: 59.5 us; the launch traced here: 59.4 us
  Pallas kernels  58.8 us (99%)
  between operations  0.64 us (1%)
    pallas_call x1, Pallas kernels, local(): pl.pallas_call(functools.partial(kernel, nz, nh, heads), out_shape=(big_b...  56.7 us
    pallas_call x1, Pallas kernels, local(): pl.pallas_call(functools.partial(finish_kernel, heads // CHUNKS), out_sha...  2.07 us

profile of v6, /device:TPU:8, one launch (start us, length us, event | category | flops | bytes accessed | tf_op | source)
XLA Modules:
  0.0 59.4 jit_solution(4656795596134328685)
XLA Ops:
  0.6 56.7 %linear_attention.1 = (bf16[512,1024]{1,0:T(8,128)(2,1)S(1)}, bf16[512,1024]{1,0:T(8,128)(2,1)S(1)}, bf16[512,1024]{1,0:T(8,128)(2,1)S(1)}, bf16[512,1024]{1,0:T...) custom-call(bf16[512,1024]{1,0:T(8,128)(2,1)} %q_hbm.1, ...), custom_call_target="tpu_custom_call" | custom-call | tf_op jit(solution)/shard_map/linear_attention/pallas_call | solution.py:486
  57.3 2.1 %key_value_grads.1 = (bf16[512,1024]{1,0:T(8,128)(2,1)}, bf16[512,1024]{1,0:T(8,128)(2,1)}, bf16[512,1024]{1,0:T(8,128)(2,1)}, bf16[512,1024]{1,0:T(8,128)(2,1)}) custom-call(bf16[512,1024]{1,0:T(8,128)(2,1)S(1)} %get-tuple-element.13.normed, bf16[512,1024]{1,0:T(8,128)(2,1)S(1)} %get-tuple-element.14.qgrad, bf16[512,1024]{1,0:T(8,128)(2,1)S(1)} %get-tuple-element.15.kgrad, ...), custom_call_target="tpu_custom_call" | custom-call | tf_op jit(solution)/shard_map/key_value_grads/pallas_call | solution.py:502

commit v7 on v6

--- a/solution.py
+++ b/solution.py
@@ -318,17 +318,17 @@
             att[:, lanes(h)] = a
             sq = sq + a * a
             pr = pr + a * grad_norm[:, lanes(h)]
-        squares[...], products[...] = sq, pr
+        if c != ARRIVAL[-1]:
+            squares[...], products[...] = sq, pr
 
     row = lax.broadcasted_iota(jnp.int32, (8, HD), 0)
     groups = BLK // HD
     packed = jnp.zeros((8, HD), F32)
     for t in range(groups):
-        part = pl.ds(t * HD, HD)
-        for first, totals in ((0, squares), (groups, products)):
+        for first, totals in ((0, sq), (groups, pr)):
             pick = (row == first + t).astype(BF16)
             packed = packed + dot_nt(
-                jnp.concatenate([pick, pick], axis=1), jnp.concatenate(split(totals[part, :], 2), axis=1)
+                jnp.concatenate([pick, pick], axis=1), jnp.concatenate(split(totals[t * HD : (t + 1) * HD], 2), axis=1)
             )
     head_src[...] = packed
     head_copies = []

time: 59.5 us -> 59.5 us (level)
  no operation moved by 1% of the time
where the time goes in v7:
time: 59.5 us; the launch traced here: 59.4 us
  Pallas kernels  58.8 us (99%)
  between operations  0.64 us (1%)
    pallas_call x1, Pallas kernels, local(): pl.pallas_call(functools.partial(kernel, nz, nh, heads), out_shape=(big_b...  56.7 us
    pallas_call x1, Pallas kernels, local(): pl.pallas_call(functools.partial(finish_kernel, heads // CHUNKS), out_sha...  2.07 us

profile of v7, /device:TPU:8, one launch (start us, length us, event | category | flops | bytes accessed | tf_op | source)
XLA Modules:
  0.0 59.4 jit_solution(4656795596134328685)
XLA Ops:
  0.6 56.7 %linear_attention.1 = (bf16[512,1024]{1,0:T(8,128)(2,1)S(1)}, bf16[512,1024]{1,0:T(8,128)(2,1)S(1)}, bf16[512,1024]{1,0:T(8,128)(2,1)S(1)}, bf16[512,1024]{1,0:T...) custom-call(bf16[512,1024]{1,0:T(8,128)(2,1)} %q_hbm.1, ...), custom_call_target="tpu_custom_call" | custom-call | tf_op jit(solution)/shard_map/linear_attention/pallas_call | solution.py:486
  57.3 2.1 %key_value_grads.1 = (bf16[512,1024]{1,0:T(8,128)(2,1)}, bf16[512,1024]{1,0:T(8,128)(2,1)}, bf16[512,1024]{1,0:T(8,128)(2,1)}, bf16[512,1024]{1,0:T(8,128)(2,1)}) custom-call(bf16[512,1024]{1,0:T(8,128)(2,1)S(1)} %get-tuple-element.13.normed, bf16[512,1024]{1,0:T(8,128)(2,1)S(1)} %get-tuple-element.14.qgrad, bf16[512,1024]{1,0:T(8,128)(2,1)S(1)} %get-tuple-element.15.kgrad, ...), custom_call_target="tpu_custom_call" | custom-call | tf_op jit(solution)/shard_map/key_value_grads/pallas_call | solution.py:502
